TPU v7x, 512 devices: a whole 4x4x16 slice. The times are simulated.
512 devices in a mesh: paths: 8 (over y, core), tm: 64 (over z, x).
Axes of the slice: x: 4, y: 4, z: 16, core: 2. Of those that a mesh axis runs over, the one named last changes fastest.
Arguments:
- independent_disturbances: bfloat16 [4096, 32, 1024], P('tm', 'paths'), may hold values from -6 to 6
- starting_driver_values: float32 [32, 1024], P('paths'), may hold values from -6 to 6
- correlation_mixer: bfloat16 [1024, 1024], P('paths'), may hold values from -0.1875 to 0.1875
- log_persistence: float32 [1024], replicated, may hold values from -0.034 to 0
- regime_multiplier: float32 [4096], P('tm'), may hold values from 0.5 to 1
- payoff_per_unit_table: bfloat16 [1024, 128], replicated, may hold values from -0.1875 to 0.1875
- short_yield_coefficients: bfloat16 [1024], replicated, may hold values from -0.1875 to 0.1875
Outputs:
- values: float32 [32, 128], P('paths')
All inputs are finite; a program needn't handle non-finite values.
Results may differ from a plain program's by a relative error of at most 0.0004.
Values may be sent and summed in bfloat16 or wider, within the bound.
A program may use at most 64 MiB of HBM per device.

v0:
```python
import jax
import jax.numpy as jnp
from jax import lax
from jax.sharding import Mesh
from jax.sharding import PartitionSpec as P

TM = ("tm_0", "tm_1")


def filled_with(shard, identity):
    return jax.tree.map(
        lambda a, e: jnp.broadcast_to(jnp.asarray(e, a.dtype), a.shape), shard, identity
    )


def all_in_one(shard, axis):
    leaves = jax.tree.leaves(shard)
    sequence = sorted(range(len(leaves)), key=lambda k: -leaves[k].size)
    width = (1, *leaves[sequence[0]].shape)[-1]
    lines = [
        jnp.pad(leaves[k].reshape(-1), (0, -leaves[k].size % width)).reshape(-1, width)
        for k in sequence
    ]
    both, at, found = (lax.all_gather(jnp.concatenate(lines), axis), 0, {})
    for k, line in zip(sequence, lines):
        piece = both[:, at : at + len(line)].reshape(len(both), -1)
        found[k] = piece[:, : leaves[k].size].reshape(-1, *leaves[k].shape)
        at += len(line)
    numbers = iter(range(len(leaves)))
    return jax.tree.map(lambda _: found[next(numbers)], shard)


def carried_in(shard, axes, combine, identity):
    before = start = filled_with(shard, identity)
    running = shard
    for axis in reversed(axes):
        peers, here = (lax.axis_size(axis), lax.axis_index(axis))
        pieces = all_in_one(running, axis)
        inside, running = (start, start)
        for k in range(peers):
            passed = k < here
            running = combine(running, jax.tree.map(lambda part: part[k], pieces))
            inside = jax.tree.map(lambda new, old: jnp.where(passed, new, old), running, inside)
        before = combine(inside, before)
    return before


def copy_for_each(shard, axis):
    copies = jnp.broadcast_to(shard, (lax.axis_size(axis), *shard.shape))
    return lax.all_to_all(copies, axis, split_axis=0, concat_axis=0, tiled=True)


def combined_pairwise(pieces, combine):
    while len(jax.tree.leaves(pieces)[0]) > 1:
        pieces = jax.vmap(combine)(*(pieces[side::2] for side in (0, 1)))
    return pieces[0]


def prefix(shard, axis, combine, identity):
    peers, here = (lax.axis_size(axis), lax.axis_index(axis))
    passed = jnp.arange(peers) < here

    def kept(part, zero, own):
        part = jnp.where(
            passed.reshape(-1, *(1 for _ in own.shape)), part, jnp.asarray(zero, own.dtype)
        )
        return part

    pieces = copy_for_each(shard, axis)
    return combined_pairwise(kept(pieces, identity, shard), combine)


def of_everyone(shard, axis):
    return copy_for_each(shard, axis).sum(axis=0)


def local(
    independent_disturbances,
    starting_driver_values,
    correlation_mixer,
    log_persistence,
    regime_multiplier,
    payoff_per_unit_table,
    short_yield_coefficients,
):
    slab_days, group_paths, driver_value_history = independent_disturbances.shape
    where_now = lax.axis_index(TM)
    correlated_disturbances = jnp.einsum(
        "spf,fg->spg",
        independent_disturbances,
        lax.all_gather(correlation_mixer, "paths", axis=0, tiled=True),
        preferred_element_type=jnp.float32,
    )
    persistence_multiplier = jnp.exp(log_persistence)
    vol = jnp.sqrt(-jnp.expm1(2.0 * log_persistence))
    leading_element = jnp.where(
        where_now == 0, starting_driver_values, jnp.zeros_like(starting_driver_values)
    )

    def propagate_one_day(carry, operand_tensors):
        state, decay = carry
        random_normal_sample, regime_multiplier_today = operand_tensors
        driver_value_now = persistence_multiplier * regime_multiplier_today
        state = driver_value_now * state + vol * random_normal_sample
        decay = decay * driver_value_now
        return ((state, decay), (state, decay))

    (state, decay), (local_states, local_decays) = lax.scan(
        propagate_one_day,
        (leading_element, jnp.ones((driver_value_history,), jnp.float32)),
        (correlated_disturbances, regime_multiplier),
    )

    def chain(earlier, later):
        return (earlier[0] * later[0], later[0][None, :] * earlier[1] + later[1])

    identity = (
        jnp.ones((driver_value_history,), jnp.float32),
        jnp.zeros((group_paths, driver_value_history), jnp.float32),
    )
    carried = carried_in((decay, state), TM, chain, identity)
    driver_trajectory = local_states + local_decays[:, None, :] * carried[1][None, :, :]
    scenario = driver_trajectory.astype(jnp.bfloat16)
    horizon_days = slab_days * lax.axis_size(TM)
    cash = jnp.einsum(
        "tpf,fk->tpk", scenario, payoff_per_unit_table, preferred_element_type=jnp.float32
    )
    rate = 0.03 + 0.3 * jnp.einsum(
        "tpf,f->tp", scenario, short_yield_coefficients, preferred_element_type=jnp.float32
    )
    running = jnp.cumsum(rate, axis=0)

    def added(earlier, later):
        return earlier + later

    before = prefix(running[-1], TM, added, jnp.zeros((group_paths,), jnp.float32))
    discount = jnp.exp(-(1.0 / 256.0) * (before[None, :] + running))
    partial_sum = jnp.sum(discount[:, :, None] * cash, axis=0) / horizon_days
    return of_everyone(partial_sum, TM)


def solution(mesh):
    split = Mesh(mesh.devices.reshape(mesh.shape["paths"], 16, 4), ("paths", "tm_0", "tm_1"))
    placed = (P(TM, "paths", None), P("paths", None), P("paths", None), P(), P(TM), P(), P())
    return jax.shard_map(
        local, mesh=split, in_specs=placed, out_specs=P("paths", None), check_vma=False
    )
```

profile of v0, /device:TPU:2, one launch (start us, length us, event | category | flops | bytes accessed | tf_op | source)
XLA Modules:
  0.0 236.4 jit_solution(2021905275992335647)
XLA Ops:
  6.5 0.7 all-gather.6.cloned.1.call-update
  7.3 0.7 reshape.283
  8.0 0.7 negate_sqrt_fusion
  8.8 38.1 %all-gather.6.cloned.1.call-done = bf16[1024,1024]{1,0:T(8,128)(2,1)} async-done(((bf16[128,1024]{1,0:T(8,128)(2,1)}), bf16[1024,1024]{1,0:T(8,128)(2,1)}) %all-gather.6.cloned.1.call-update) | async-done | bytes 2097168 | tf_op jit(solution)/shard_map/all_gather | solution.py:91
  46.9 2.5 %fusion.2 = f32[64,4,1024]{2,0,1:T(8,128)S(1)} fusion(bf16[1024,1024]{1,0:T(8,128)(2,1)} %all-gather.6.cloned.1.call-done, bf16[64,4,1024]{2,1,0:T(4,128)(2,1)} %param.9), kind=kOutput, calls=%fused_computation.7 | convolution fusion | flops 536870912 | bytes 3670016 | tf_op jit(solution)/shard_map/spf,fg->spg/dot_general | solution.py:88
  49.4 85.9 %while.17 = (s32[]{:T(128)}, f32[4,1024]{1,0:T(4,128)S(1)}, f32[1024]{0:T(1024)S(1)}, f32[64,4,1024]{2,1,0:T(4,128)S(1)}, f32[64,1024]{1,0:T(8,128)S(1)}, /*inde...) while((s32[]{:T(128)}, f32[4,1024]{1,0:T(4,128)S(1)}, ...), condition=%wide.region_1.2_spmd.clone, body=%wide.region_0.1_spmd.clone.sunk | while | flops 15363 | bytes 131219 | solution.py:108
  49.4 0.6 dynamic_slice.14
  50.7 0.6 dynamic_slice.14
  52.1 0.6 dynamic_slice.14
  54.7 0.6 dynamic_slice.14
  57.4 0.6 dynamic_slice.14
  58.8 0.6 dynamic_slice.14
  60.1 0.6 dynamic_slice.14
  61.5 0.6 dynamic_slice.14
  64.1 0.6 dynamic_slice.14
  66.8 0.6 dynamic_slice.14
  68.2 0.6 dynamic_slice.14
  135.3 12.2 %all-gather.2 = f32[4,5,1024]{2,1,0:T(8,128)S(1)} all-gather(f32[1,5,1024]{2,1,0:T(8,128)S(1)} %maximum_bitcast_fusion), channel_id=2, replica_groups=mesh['paths'=8,'tm_0'=16,'tm_1'=4] {'tm_1'}, dimensions={0}, use_global_device_ids=true | all-gather | bytes 102400 | tf_op jit(solution)/shard_map/all_gather | solution.py:24
  147.6 33.2 %all-gather.3 = f32[16,5,1024]{2,1,0:T(8,128)S(1)} all-gather(f32[1,5,1024]{2,1,0:T(8,128)S(1)} %maximum_bitcast_fusion.1), channel_id=3, replica_groups=mesh['paths'=8,'tm_0'=16,'tm_1'=4] {'tm_0'}, dimensions={0}, use_global_device_ids=true | all-gather | bytes 348160 | tf_op jit(solution)/shard_map/all_gather | solution.py:24
  181.9 0.6 broadcast_in_dim.41
  182.5 11.7 %all-to-all-start = ((f32[64,1,4]{2,1,0:T(1,128)}), f32[64,1,4]{2,1,0:T(1,128)S(1)}, u32[]{:S(2)}, u32[]{:S(2)}) async-start(f32[64,1,4]{2,1,0:T(1,128)} %broadcast_in_dim.41), calls=%async_computation | async-start | bytes 65536 | tf_op jit(solution)/shard_map/all_to_all | solution.py:50
  194.3 13.8 %all-to-all-done = f32[64,1,4]{2,1,0:T(1,128)S(1)} async-done(((f32[64,1,4]{2,1,0:T(1,128)}), f32[64,1,4]{2,1,0:T(1,128)S(1)}, u32[]{:S(2)}, u32[]{:S(2)}) %all-to-all-start) | async-done | bytes 1056 | tf_op jit(solution)/shard_map/all_to_all | solution.py:50
  208.8 20.1 %all_to_all.14 = f32[64,4,128]{2,1,0:T(4,128)S(1)} all-to-all(f32[64,4,128]{2,1,0:T(4,128)S(1)} %broadcast_in_dim.43), channel_id=1, replica_groups=mesh['paths'=8,'tm_0'=16,'tm_1'=4] {'tm_0','tm_1'}, dimensions={0} | all-to-all | bytes 262144 | tf_op jit(solution)/shard_map/all_to_all | solution.py:50
  228.9 0.7 reduce_sum.19
  (354 shorter events, 78.8 us)
Async XLA Ops:
  6.5 201.9 %copy-start = (bf16[1024,128]{1,0:T(8,128)(2,1)S(1)}, bf16[1024,128]{1,0:T(8,128)(2,1)}, u32[]{:S(2)}) copy-start(bf16[1024,128]{1,0:T(8,128)(2,1)} %param.14) | copy-start | bytes 786436
  6.5 42.8 %copy-start.1 = (f32[64]{0:T(128)S(1)}, f32[64]{0:T(128)}, u32[]{:S(2)}) copy-start(f32[64]{0:T(128)} %param.13) | copy-start | bytes 772
  6.5 40.3 %all-gather.6.cloned.1.call-start = ((), (), s32[]{:S(2)}) async-start(), calls=%async_computation.2 | async-start | bytes 2359296 | tf_op jit(solution)/shard_map/all_gather | solution.py:91
  182.5 25.5 %all-to-all-start = ((f32[64,1,4]{2,1,0:T(1,128)}), f32[64,1,4]{2,1,0:T(1,128)S(1)}, u32[]{:S(2)}, u32[]{:S(2)}) async-start(f32[64,1,4]{2,1,0:T(1,128)} %broadcast_in_dim.41), calls=%async_computation | async-start | bytes 65536 | tf_op jit(solution)/shard_map/all_to_all | solution.py:50
Sparse Core Ops, SparseCore 0:
  9.5 37.2 all-gather.5
where the time goes:
time: 237 us; the launch traced here: 236 us
  blocking collectives  65.5 us (28%)
  waiting for transfers between devices  52.6 us (22%)
  local copies, waits for them, and re-layouts  47.2 us (20%)
  other arithmetic  39.9 us (17%)
  between operations  13.6 us (6%)
  starting transfers between devices  11.7 us (5%)
  matrix products  3.15 us (1%)
  loops' own time  2.69 us (1%)
    all_gather x2, blocking collectives, all_in_one(): both, at, found = (lax.all_gather(jnp.concatenate(lines), axis), 0, {})  45.4 us
    dynamic_slice x128, local copies, waits for them, and re-layouts, local(): lax.scan(propagate_one_day, (leading_element, jnp.ones((driver_value_hist...  38.5 us
    all_gather x1, waiting for transfers between devices, local(): lax.all_gather(correlation_mixer, 'paths', axis=0, tiled=True)  38.1 us
    mul x64, other arithmetic, propagate_one_day(): decay = decay * driver_value_now  36 us
    all_to_all x1, blocking collectives, copy_for_each(): return lax.all_to_all(copies, axis, split_axis=0, concat_axis=0, tiled=True)  20.1 us
    all_to_all x1, waiting for transfers between devices, copy_for_each(): return lax.all_to_all(copies, axis, split_axis=0, concat_axis=0, tiled=True)  13.8 us
    all_to_all x1, starting transfers between devices, copy_for_each(): return lax.all_to_all(copies, axis, split_axis=0, concat_axis=0, tiled=True)  11.7 us
    dynamic_update_slice x64, local copies, waits for them, and re-layouts, local(): lax.scan(propagate_one_day, (leading_element, jnp.ones((driver_value_hist...  7.04 us
  transfers between devices with their start and end apart: 2, of which 2 were waited for; matrix products, arithmetic and copies ran while one was open for 1% of the time, Pallas kernels for 0%

commit v1 on v0

--- a/solution.py
+++ b/solution.py
@@ -5,6 +5,13 @@
 from jax.sharding import PartitionSpec as P
 
 TM = ("tm_0", "tm_1")
+
+
+def swapped_in(x, name, dim):
+    size = lax.axis_size(name)
+    shards = jnp.stack([x for _ in range(size)])
+    shards = lax.all_to_all(shards, name, split_axis=0, concat_axis=0)
+    return jnp.concatenate(shards, axis=dim)
 
 
 def filled_with(shard, identity):
@@ -88,7 +95,7 @@
     correlated_disturbances = jnp.einsum(
         "spf,fg->spg",
         independent_disturbances,
-        lax.all_gather(correlation_mixer, "paths", axis=0, tiled=True),
+        swapped_in(correlation_mixer, "paths", 0),
         preferred_element_type=jnp.float32,
     )
     persistence_multiplier = jnp.exp(log_persistence)

time: 237 us -> 356 us (1.50); the launches traced: 236 us -> 351 us
  local copies, waits for them, and re-layouts: 47.2 us -> 135 us
  other arithmetic: 39.9 us -> 85.8 us
  between operations: 13.6 us -> 0.25 us
  waiting for transfers between devices: 52.6 us -> 40.6 us
  blocking collectives: 65.5 us -> 70.8 us
    dynamic_update_slice x64, local copies, waits for them, and re-layouts: 7.04 us -> 88.5 us  [local(): lax.scan(propagate_one_day, (leading_element, jnp.ones((driver_value_hist...]
    all_gather x1 -> x0, waiting for transfers between devices: 38.1 us -> none  [local(): lax.all_gather(correlation_mixer, 'paths', axis=0, tiled=True)]
    dynamic_update_slice x64, other arithmetic: 1.72 us -> 39.6 us  [local(): lax.scan(propagate_one_day, (leading_element, jnp.ones((driver_value_hist...]
    all_to_all x0 -> x1, waiting for transfers between devices: none -> 27 us  [swapped_in(): shards = lax.all_to_all(shards, name, split_axis=0, concat_axis=0)]
    mul x64, other arithmetic: 36 us -> 43.8 us  [propagate_one_day(): decay = decay * driver_value_now]
    all_gather x2, blocking collectives: 45.4 us -> 50.5 us  [all_in_one(): both, at, found = (lax.all_gather(jnp.concatenate(lines), axis), 0, {})]
    all_to_all x0 -> x1, starting transfers between devices: none -> 4.6 us  [swapped_in(): shards = lax.all_to_all(shards, name, split_axis=0, concat_axis=0)]
    dynamic_slice x128, local copies, waits for them, and re-layouts: 38.5 us -> 43.1 us  [local(): lax.scan(propagate_one_day, (leading_element, jnp.ones((driver_value_hist...]
  transfers between devices with their start and end apart: 2 -> 2, of which waited for: 2 -> 2; matrix products, arithmetic and copies ran while one was open for 1% -> 0% of each run, Pallas kernels for 0% -> 0%
where the time goes in v1:
time: 356 us; the launch traced here: 351 us
  local copies, waits for them, and re-layouts  135 us (38%)
  other arithmetic  85.8 us (24%)
  blocking collectives  70.8 us (20%)
  waiting for transfers between devices  40.6 us (11%)
  starting transfers between devices  14.4 us (4%)
    dynamic_update_slice x64, local copies, waits for them, and re-layouts, local(): lax.scan(propagate_one_day, (leading_element, jnp.ones((driver_value_hist...  88.5 us
    all_gather x2, blocking collectives, all_in_one(): both, at, found = (lax.all_gather(jnp.concatenate(lines), axis), 0, {})  50.5 us
    mul x64, other arithmetic, propagate_one_day(): decay = decay * driver_value_now  43.8 us
    dynamic_slice x128, local copies, waits for them, and re-layouts, local(): lax.scan(propagate_one_day, (leading_element, jnp.ones((driver_value_hist...  43.1 us
    dynamic_update_slice x64, other arithmetic, local(): lax.scan(propagate_one_day, (leading_element, jnp.ones((driver_value_hist...  39.6 us
    all_to_all x1, waiting for transfers between devices, swapped_in(): shards = lax.all_to_all(shards, name, split_axis=0, concat_axis=0)  27 us
    all_to_all x1, blocking collectives, copy_for_each(): return lax.all_to_all(copies, axis, split_axis=0, concat_axis=0, tiled=True)  20.3 us
    all_to_all x1, waiting for transfers between devices, copy_for_each(): return lax.all_to_all(copies, axis, split_axis=0, concat_axis=0, tiled=True)  13.6 us
  transfers between devices with their start and end apart: 2, of which 2 were waited for; matrix products, arithmetic and copies ran while one was open for 0% of the time, Pallas kernels for 0%

profile of v1, /device:TPU:2, one launch (start us, length us, event | category | flops | bytes accessed | tf_op | source)
XLA Modules:
  0.0 350.7 jit_solution(5470583980798373335)
XLA Ops:
  0.0 2.6 stack.2
  2.6 4.6 %all-to-all-start = ((bf16[8,128,1024]{2,1,0:T(8,128)(2,1)}), bf16[8,128,1024]{2,1,0:T(8,128)(2,1)S(1)}, u32[]{:S(2)}, u32[]{:S(2)}) async-start(bf16[8,128,1024]{2,1,0:T(8,128)(2,1)} %stack.2), calls=%async_computation | async-start | bytes 4194304 | tf_op jit(solution)/shard_map/all_to_all | solution.py:13
  7.4 27.0 %all-to-all-done = bf16[8,128,1024]{2,1,0:T(8,128)(2,1)S(1)} async-done(((bf16[8,128,1024]{2,1,0:T(8,128)(2,1)}), bf16[8,128,1024]{2,1,0:T(8,128)(2,1)S(1)}, u32[]{:S(2)}, u32[]{:S(2)}) %all-to-all-start) | async-done | bytes 2097184 | tf_op jit(solution)/shard_map/all_to_all | solution.py:13
  34.4 1.8 fusion.3
  36.2 216.0 %while.17 = (s32[]{:T(128)}, f32[4,1024]{1,0:T(4,128)S(1)}, f32[1024]{0:T(1024)S(1)}, f32[64,4,1024]{2,1,0:T(4,128)}, f32[64,1024]{1,0:T(8,128)}, /*index=5*/f32...) while((s32[]{:T(128)}, f32[4,1024]{1,0:T(4,128)S(1)}, ...), condition=%wide.region_1.2_spmd.clone, body=%wide.region_0.1_spmd.clone.sunk | while | flops 15363 | bytes 131727 | solution.py:115
  38.2 1.4 dynamic_update_slice.14
  41.6 1.4 dynamic_update_slice.14
  45.0 1.4 dynamic_update_slice.14
  48.4 1.4 dynamic_update_slice.14
  51.8 1.4 dynamic_update_slice.14
  55.2 1.4 dynamic_update_slice.14
  58.5 1.4 dynamic_update_slice.14
  61.9 1.4 dynamic_update_slice.14
  200.3 1.4 dynamic_update_slice.14
  203.6 1.4 dynamic_update_slice.14
  207.0 1.4 dynamic_update_slice.14
  210.4 1.4 dynamic_update_slice.14
  213.8 1.4 dynamic_update_slice.14
  217.2 1.4 dynamic_update_slice.14
  252.3 13.9 %all-gather.2 = f32[4,5,1024]{2,1,0:T(8,128)S(1)} all-gather(f32[1,5,1024]{2,1,0:T(8,128)S(1)} %maximum_bitcast_fusion), channel_id=2, replica_groups=mesh['paths'=8,'tm_0'=16,'tm_1'=4] {'tm_1'}, dimensions={0}, use_global_device_ids=true | all-gather | bytes 102400 | tf_op jit(solution)/shard_map/all_gather | solution.py:31
  266.2 36.7 %all-gather.3 = f32[16,5,1024]{2,1,0:T(8,128)S(1)} all-gather(f32[1,5,1024]{2,1,0:T(8,128)S(1)} %maximum_bitcast_fusion.1), channel_id=3, replica_groups=mesh['paths'=8,'tm_0'=16,'tm_1'=4] {'tm_0'}, dimensions={0}, use_global_device_ids=true | all-gather | bytes 348160 | tf_op jit(solution)/shard_map/all_gather | solution.py:31
  305.6 9.8 %all-to-all-start.1 = ((f32[64,1,4]{2,1,0:T(1,128)}), f32[64,1,4]{2,1,0:T(1,128)S(1)}, u32[]{:S(2)}, u32[]{:S(2)}) async-start(f32[64,1,4]{2,1,0:T(1,128)} %broadcast_in_dim.41), calls=%async_computation.1 | async-start | bytes 65536 | tf_op jit(solution)/shard_map/all_to_all | solution.py:57
  315.4 13.6 %all-to-all-done.1 = f32[64,1,4]{2,1,0:T(1,128)S(1)} async-done(((f32[64,1,4]{2,1,0:T(1,128)}), f32[64,1,4]{2,1,0:T(1,128)S(1)}, u32[]{:S(2)}, u32[]{:S(2)}) %all-to-all-start.1) | async-done | bytes 1056 | tf_op jit(solution)/shard_map/all_to_all | solution.py:57
  329.8 20.3 %all_to_all.19 = f32[64,4,128]{2,1,0:T(4,128)S(1)} all-to-all(f32[64,4,128]{2,1,0:T(4,128)S(1)} %broadcast_in_dim.43), channel_id=1, replica_groups=mesh['paths'=8,'tm_0'=16,'tm_1'=4] {'tm_0','tm_1'}, dimensions={0} | all-to-all | bytes 262144 | tf_op jit(solution)/shard_map/all_to_all | solution.py:57
  (362 shorter events, 199.7 us)
Async XLA Ops:
  0.0 329.4 %copy-start = (bf16[1024,128]{1,0:T(8,128)(2,1)S(1)}, bf16[1024,128]{1,0:T(8,128)(2,1)}, u32[]{:S(2)}) copy-start(bf16[1024,128]{1,0:T(8,128)(2,1)} %param.14) | copy-start | bytes 786436
  2.6 4.7 %copy-start.4 = (bf16[1024]{0:T(1024)(128)(2,1)S(1)}, bf16[1024]{0:T(1024)(128)(2,1)}, u32[]{:S(2)}) copy-start(bf16[1024]{0:T(1024)(128)(2,1)} %param.15) | copy-start | bytes 6148
  2.6 4.7 %copy-start.3 = (f32[1024]{0:T(1024)S(1)}, f32[1024]{0:T(1024)}, u32[]{:S(2)}) copy-start(f32[1024]{0:T(1024)} %param.12) | copy-start | bytes 12292
  2.6 4.7 %copy-start.2 = (f32[4,1024]{1,0:T(4,128)S(1)}, f32[4,1024]{1,0:T(4,128)}, u32[]{:S(2)}) copy-start(f32[4,1024]{1,0:T(4,128)} %param.10) | copy-start | bytes 49156
  2.6 31.8 %all-to-all-start = ((bf16[8,128,1024]{2,1,0:T(8,128)(2,1)}), bf16[8,128,1024]{2,1,0:T(8,128)(2,1)S(1)}, u32[]{:S(2)}, u32[]{:S(2)}) async-start(bf16[8,128,1024]{2,1,0:T(8,128)(2,1)} %stack.2), calls=%async_computation | async-start | bytes 4194304 | tf_op jit(solution)/shard_map/all_to_all | solution.py:13
  7.2 29.0 %copy-start.5 = (f32[64]{0:T(128)S(1)}, f32[64]{0:T(128)}, u32[]{:S(2)}) copy-start(f32[64]{0:T(128)} %param.13) | copy-start | bytes 772
  252.3 50.9 %copy-start.1 = (f32[64,4,1024]{2,1,0:T(4,128)S(1)}, f32[64,4,1024]{2,1,0:T(4,128)}, u32[]{:S(2)}) copy-start(f32[64,4,1024]{2,1,0:T(4,128)} %get-tuple-element.55) | copy-start | bytes 3145732
  305.6 23.4 %all-to-all-start.1 = ((f32[64,1,4]{2,1,0:T(1,128)}), f32[64,1,4]{2,1,0:T(1,128)S(1)}, u32[]{:S(2)}, u32[]{:S(2)}) async-start(f32[64,1,4]{2,1,0:T(1,128)} %broadcast_in_dim.41), calls=%async_computation.1 | async-start | bytes 65536 | tf_op jit(solution)/shard_map/all_to_all | solution.py:57
